TPU v7x, 128 devices: a whole 4x4x4 slice. The times are simulated.
128 devices in a mesh: ctx: 16 (over z, x_lo, core), fsdp: 8 (over x_hi, y).
Axes of the slice: x: 4 (x_hi: 2, x_lo: 2; x = x_hi * 2 + x_lo), y: 4, z: 4, core: 2. Of those that a mesh axis runs over, the one named last changes fastest.
Arguments:
- inputs: bfloat16 [8192, 5376], P('ctx'), may hold values from -400 to 400
- output_cotangent: bfloat16 [8192, 4096], P('ctx', 'fsdp'), may hold values from -96 to 96
- w_query: bfloat16 [5376, 4096], P('ctx', 'fsdp'), may hold values from -0.078125 to 0.078125
- key_projection: bfloat16 [5376, 2048], P('ctx', 'fsdp'), may hold values from -0.078125 to 0.078125
- value_projection: bfloat16 [5376, 2048], P('ctx', 'fsdp'), may hold values from -0.078125 to 0.078125
- norm_gain: float32 [5376], replicated, may hold values from 0.25 to 1.75
- q_gain: float32 [128], replicated, may hold values from 0.25 to 1.75
- key_norm_gain: float32 [128], replicated, may hold values from 0.25 to 1.75
- half_lengths: int32 [4], replicated, may hold values from 1 to 6144, 8192 in all
Outputs:
- grad_inputs: bfloat16 [8192, 5376], P('ctx', 'fsdp')
- grad_w_query: bfloat16 [5376, 4096], P('ctx', 'fsdp')
- grad_w_key: bfloat16 [5376, 2048], P('ctx', 'fsdp')
- grad_w_value: bfloat16 [5376, 2048], P('ctx', 'fsdp')
- grad_norm_gain: float32 [5376], P(('fsdp', 'ctx'))
- grad_q_gain: float32 [128], replicated
- grad_k_gain: float32 [128], replicated
- norm_row_dots: float32 [8192], P('ctx')
Inputs may be any that keep to these rules, and one draw needn't show every extreme that they name: `half_lengths`: the halves add up to 8192 tokens, and the longest holds exactly 6144.
All inputs are finite; a program needn't handle non-finite values.
Results may differ from a plain program's by a relative error of at most 0.035.
Values may be sent and summed in bfloat16 or wider, within the bound.
A program may use at most 128 MiB of HBM per device.

v0:
```python
import jax
import jax.numpy as jnp
from jax import lax
from jax.experimental import pallas as pl
from jax.experimental.pallas import tpu as pltpu
from jax.sharding import PartitionSpec as P

WIN = 1024
REACH = 2


epsilon = 1e-06
query_scale = 168.0 ** (-0.5)


F32, BF16 = jnp.float32, jnp.bfloat16
NT = (((1,), (1,)), ((), ()))
TN = (((0,), (0,)), ((), ()))
MESH = pl.DeviceIdType.MESH
LOG2E = 1.4426950408889634


def attention_and_reductions(w_ref, nt_ref, nt_far_ref, q_ref, kv_ref, do_ref, lo_ref, proj_ref, q_mul_ref, k_mul_ref,
                             x_mine_ref, inv_ref, scale, q_scale):
    tokens, q_cols = q_ref.shape
    cols = proj_ref.shape[1]
    part = w_ref.shape[1] // 16
    wing = cols // 2
    kvs = kv_ref.shape[1] // 2
    head = q_mul_ref.shape[1]
    kv_heads = kvs // head
    group = q_cols // kvs
    half = tokens // 2
    span = 5 * half
    reach = kv_ref.shape[0]
    quarter = tokens // 2

    def kernel(w_hbm, nt_hbm, nt_far_hbm, q, kv, do, lo, proj, q_mul, k_mul, x_mine, inv,
               dn_out, wg_out, sum_f, sum_c,
               w, nt, nt_far, v_one, e_all, mask, dkey, dval, kvg, kvg_in, own_kv, d, d_far, small,
               slots_f, slots_c, mine_c, far, near, far_in, near_in, cross, cross_in,
               fetch_sem, kvg_s, kvg_r, swap_s, swap_r, few_s, few_r, far_s, far_r, near_s, near_r, cross_s, cross_r):
        c, f = lax.axis_index("ctx"), lax.axis_index("fsdp")
        z, x, core = c // 4, lax.rem(c // 2, 2), lax.rem(c, 2)
        xh, y = f // 4, lax.rem(f, 4)
        ring = (
            lambda k: (c, xh * 4 + lax.rem(y + k, 4)),
            lambda k: (lax.rem(z + k, 4) * 4 + x * 2 + core, f),
        )
        across = ((c, (1 - xh) * 4 + y), (z * 4 + (1 - x) * 2 + core, f))
        twin = (z * 4 + x * 2 + 1 - core, f)
        peers_f = [(c, lax.rem(f + k, 8)) for k in range(1, 8)]
        peers_c = [(lax.rem(c + k, 16), f) for k in range(1, 16)]

        def rows_of(block):
            return pl.ds(pl.multiple_of(block * part, 16), part)

        barrier = pltpu.get_barrier_semaphore()
        partners = peers_f + peers_c
        for partner in partners:
            pl.semaphore_signal(barrier, inc=1, device_id=partner, device_id_type=MESH)
        fetches = [pltpu.make_async_copy(nt_hbm.at[rows_of(j * 2 + core)], nt.at[j], fetch_sem.at[j]) for j in range(8)]
        fetches.append(pltpu.make_async_copy(nt_far_hbm, nt_far, fetch_sem.at[8]))
        fetches.append(pltpu.make_async_copy(w_hbm, w, fetch_sem.at[9]))
        for cp in fetches:
            cp.start()

        def copy(src, dst, ss, rs, to):
            return pltpu.make_async_remote_copy(
                src_ref=src, dst_ref=dst, send_sem=ss, recv_sem=rs, device_id=to, device_id_type=MESH
            )

        sent = []

        def go(*what):
            cp = copy(*what)
            cp.start()
            sent.append(cp)
            return cp

        ones = jnp.ones((reach, head), BF16)
        for g in range(kv_heads):
            v_one[g, :, :head] = kv[:, kvs + g * head : kvs + (g + 1) * head]
            v_one[g, :, head:] = ones
        for t in range(2):
            col = lax.broadcasted_iota(jnp.int32, (half, span), 1) + t * half
            row = lax.broadcasted_iota(jnp.int32, (half, span), 0) + t * half
            seen = (col >= lo[t * half : (t + 1) * half, :]) & (col <= row + 2 * tokens)
            mask[t] = jnp.where(seen, 1.0, 0.0).astype(BF16)
        lane = lax.broadcasted_iota(jnp.int32, (half, head), 1)

        def norm_back(grad, raw, mul):
            one = lax.rsqrt(jnp.mean(raw * raw, axis=1, keepdims=True) + epsilon)
            hat = raw * one
            up = grad * mul
            back = one * (up - hat * jnp.mean(up * hat, axis=1, keepdims=True))
            return back.astype(BF16), jnp.sum(grad * hat, axis=0, keepdims=True)

        q_term = jnp.zeros((1, head), F32)
        kv_copies = []
        for g in range(kv_heads):
            dkey[...] = jnp.zeros_like(dkey)
            dval[...] = jnp.zeros_like(dval)
            for r in range(group):
                h = g * group + r
                hc = slice(h * head, (h + 1) * head)
                for t in range(2):
                    qs = slice(t * half, (t + 1) * half)
                    ks = slice(t * half, t * half + span)
                    qt = q[qs, hc]
                    keys = kv[ks, g * head : (g + 1) * head]
                    s = lax.dot_general(qt, keys, NT, preferred_element_type=F32)
                    e_all[...] = jnp.exp2(s).astype(BF16) * mask[t]
                    out = jnp.dot(e_all[...], v_one[g, ks, :], preferred_element_type=F32)
                    inv_l = 1.0 / out[:, head:]
                    scaled = do[qs, hc].astype(F32) * inv_l
                    delta = jnp.sum(scaled * (out[:, :head] * inv_l), axis=1, keepdims=True)
                    d_hi = delta.astype(BF16).astype(F32)
                    tail = jnp.where(lane == 0, -d_hi, jnp.where(lane == 1, d_hi - delta, 0.0))
                    scaled16 = scaled.astype(BF16)
                    both = jnp.concatenate([scaled16, tail.astype(BF16)], axis=1)
                    dp = lax.dot_general(both, v_one[g, ks, :], NT, preferred_element_type=F32)
                    ds = dp.astype(BF16) * e_all[...]
                    dq = jnp.dot(ds, keys, preferred_element_type=F32)
                    dkey[ks, :] += lax.dot_general(ds, qt, TN, preferred_element_type=F32)
                    dval[ks, :] += lax.dot_general(e_all[...], scaled16, TN, preferred_element_type=F32)
                    d[qs, hc], term_q = norm_back(dq, proj[qs, hc], q_mul[...])
                    q_term += term_q
            if g == 0:
                pl.semaphore_wait(barrier, len(partners))
            for n in range(2):
                away = slice((1 - n) * tokens, (2 - n) * tokens)
                kvg[g, n, :, :head] = (dkey[away, :] * (1.0 / LOG2E)).astype(BF16)
                kvg[g, n, :, head:] = dval[away, :].astype(BF16)
                kv_copies.append(
                    go(kvg.at[g, n], kvg_in.at[g, n], kvg_s.at[g, n], kvg_r.at[g, n], (lax.rem(c + 15 - n, 16), f))
                )
            own_kv[:, g * head : (g + 1) * head] = dkey[2 * tokens :, :] * (1.0 / LOG2E)
            own_kv[:, kvs + g * head : kvs + (g + 1) * head] = dval[2 * tokens :, :]
        swap_q = go(d.at[:, pl.ds(0, wing)], d_far.at[:, pl.ds(0, wing)], swap_s.at[0], swap_r.at[0], twin)

        def term(m, s, k, h):
            if m == 0:
                block = (xh if s else 1 - xh) * 4 + lax.rem(y + k, 4)
                rows = rows_of(block * 2 + h)
                total = lax.dot_general(w[0, rows, :], d[:, :wing], NT, preferred_element_type=F32)
                total += lax.dot_general(w[1, rows, :], d[:, wing:], NT, preferred_element_type=F32)
                return total
            block = lax.rem(z + k, 4) * 2 + (x if s else 1 - x)
            hs = slice(h * wing, (h + 1) * wing)
            total = jnp.dot(nt[block], d[:, hs], preferred_element_type=F32)
            total += jnp.dot(nt_far[block], d_far[:, hs], preferred_element_type=F32)
            return total * scale

        fars, nears, crossed = {}, {}, {}

        def send_far(m, s, h):
            far[m, s, h] = term(m, s, 2, h).astype(BF16)
            for n, k in enumerate((1, 3)):
                fars[m, s, h, n] = go(
                    far.at[m, s, h, :, pl.ds(n * quarter, quarter)], far_in.at[m, s, h, n],
                    far_s.at[m, s, h, n], far_r.at[m, s, h, n], ring[m](k),
                )

        def make_near(m, s, h):
            for n, k in enumerate((1, 3)):
                near[m, s, n, h] = term(m, s, k, h).astype(BF16)

        def send_near(m, s, h):
            for n, k in enumerate((1, 3)):
                fars[m, s, h, n].wait_recv()
                at = slice(n * quarter, (n + 1) * quarter)
                near[m, s, n, h, :, at] = (
                    near[m, s, n, h, :, at].astype(F32) + far_in[m, s, h, n].astype(F32)
                ).astype(BF16)
                nears[m, s, n, h] = go(
                    near.at[m, s, n, h], near_in.at[m, s, n, h], near_s.at[m, s, n, h], near_r.at[m, s, n, h], ring[m](k)
                )

        def arrived(m, s, h):
            for n in range(2):
                nears[m, s, n, h].wait_recv()
            return near_in[m, s, 0, h].astype(F32) + near_in[m, s, 1, h].astype(F32)

        def send_cross(m, h):
            mine = term(m, 0, 0, h)
            cross[m, h] = (mine + arrived(m, 0, h)).astype(BF16)
            crossed[m, h] = go(cross.at[m, h], cross_in.at[m, h], cross_s.at[m, h], cross_r.at[m, h], across[m])

        for cp in fetches[:9]:
            cp.wait()
        swap_q.wait_recv()
        send_far(1, 0, 0)
        make_near(1, 0, 0)
        send_near(1, 0, 0)

        k_term = jnp.zeros((1, head), F32)
        for cp in kv_copies:
            cp.wait_recv()
        for g in range(kv_heads):
            at = slice(g * head, (g + 1) * head)
            there = slice(wing + g * head, wing + (g + 1) * head)
            grad = own_kv[:, at] + (kvg_in[g, 0, :, :head].astype(F32) + kvg_in[g, 1, :, :head].astype(F32))
            d[:, there], term_k = norm_back(grad, proj[:, there], k_mul[...])
            k_term += term_k
            at = slice(kvs + g * head, kvs + (g + 1) * head)
            grad = own_kv[:, at] + (kvg_in[g, 0, :, head:].astype(F32) + kvg_in[g, 1, :, head:].astype(F32))
            d[:, wing + kvs + g * head : wing + kvs + (g + 1) * head] = grad.astype(BF16)
        swap_kv = go(d.at[:, pl.ds(wing, wing)], d_far.at[:, pl.ds(wing, wing)], swap_s.at[1], swap_r.at[1], twin)
        fetches[9].wait()
        send_far(0, 0, 0)
        make_near(0, 0, 0)
        send_far(0, 0, 1)
        send_near(0, 0, 0)
        swap_kv.wait_recv()
        send_far(1, 0, 1)
        make_near(0, 0, 1)
        send_far(0, 1, 0)
        send_near(0, 0, 1)
        make_near(1, 0, 1)
        send_far(1, 1, 0)
        send_near(1, 0, 1)

        product = d[...].astype(F32) * proj[...]
        upper = product.astype(BF16)
        lower = (product - upper.astype(F32)).astype(BF16)
        ones_row = jnp.ones((8, cols), BF16)
        dots = lax.dot_general(ones_row, upper, NT, preferred_element_type=F32)
        dots += lax.dot_general(ones_row, lower, NT, preferred_element_type=F32)
        small[...] = dots
        small[1:2, :head] = q_term * (scale * q_scale)
        small[1:2, head : 2 * head] = k_term * scale
        slots_f[f] = small[...]
        few = [go(small, slots_f.at[f], few_s.at[k], few_r.at[k], to) for k, to in enumerate(peers_f)]

        send_cross(0, 0)
        make_near(0, 1, 0)
        send_far(0, 1, 1)
        send_near(0, 1, 0)
        send_cross(1, 0)
        send_cross(0, 1)
        make_near(1, 1, 0)
        send_far(1, 1, 1)
        send_near(1, 1, 0)
        send_cross(1, 1)
        make_near(0, 1, 1)
        send_near(0, 1, 1)
        make_near(1, 1, 1)
        send_near(1, 1, 1)
        for cp in few:
            cp.wait_recv()
        total_f = slots_f[0]
        for k in range(1, 8):
            total_f = total_f + slots_f[k]
        sum_f[...] = total_f
        for h in range(2):
            dn_out[h] = term(0, 1, 0, h)
        for h in range(2):
            own_kv[:part, :] = term(1, 1, 0, h)
            crossed[1, h].wait_recv()
            total = own_kv[:part, :] + cross_in[1, h].astype(F32) + arrived(1, 1, h)
            wg_out[:, h * wing : (h + 1) * wing] = total.astype(BF16)
        spread = jnp.zeros((128, 128), F32)
        for h in range(2):
            crossed[0, h].wait_recv()
            total = dn_out[h] + cross_in[0, h].astype(F32) + arrived(0, 1, h)
            dn_out[h] = total
            hat = x_mine[h * part : (h + 1) * part, :].astype(F32) * inv[...]
            sums = scale * jnp.sum(total * hat, axis=1, keepdims=True)
            at = lax.broadcasted_iota(jnp.int32, (part, 128), 0) + h * part
            lanes = lax.broadcasted_iota(jnp.int32, (part, 128), 1)
            to_row = jnp.where(at // 128 == lanes, sums, 0.0)
            to_lane = jnp.where(lax.rem(at, 128) == lanes, 1.0, 0.0)
            spread += lax.dot_general(to_row.astype(BF16), to_lane.astype(BF16), TN, preferred_element_type=F32)
        mine_c[...] = spread[:8]
        mine_c[6:7, :] = total_f[1:2, :head]
        mine_c[7:8, :] = total_f[1:2, head : 2 * head]
        slots_c[c] = mine_c[...]
        few_c = [go(mine_c, slots_c.at[c], few_s.at[7 + k], few_r.at[7 + k], to) for k, to in enumerate(peers_c)]
        for cp in few_c:
            cp.wait_recv()
        total_c = slots_c[0]
        for k in range(1, 16):
            total_c = total_c + slots_c[k]
        sum_c[...] = total_c
        for cp in sent:
            cp.wait_send()

    vm = pl.BlockSpec(memory_space=pltpu.VMEM)
    anywhere = pl.BlockSpec(memory_space=pl.ANY)
    dma = pltpu.SemaphoreType.DMA
    block = (2, part, tokens)
    return pl.pallas_call(
        kernel,
        out_shape=(
            jax.ShapeDtypeStruct(block, F32),
            jax.ShapeDtypeStruct((part, cols), BF16),
            jax.ShapeDtypeStruct((8, tokens), F32),
            jax.ShapeDtypeStruct((8, 128), F32),
        ),
        in_specs=[anywhere] * 3 + [vm] * 9,
        out_specs=(vm,) * 4,
        scratch_shapes=[
            pltpu.VMEM(w_ref.shape, BF16),
            pltpu.VMEM((8, part, tokens), BF16),
            pltpu.VMEM((8, part, tokens), BF16),
            pltpu.VMEM((kv_heads, reach, 2 * head), BF16),
            pltpu.VMEM((half, span), BF16),
            pltpu.VMEM((2, half, span), BF16),
            pltpu.VMEM((reach, head), F32),
            pltpu.VMEM((reach, head), F32),
            pltpu.VMEM((2, 2, tokens, 2 * head), BF16),
            pltpu.VMEM((2, 2, tokens, 2 * head), BF16),
            pltpu.VMEM((tokens, 2 * kvs), F32),
            pltpu.VMEM((tokens, cols), BF16),
            pltpu.VMEM((tokens, cols), BF16),
            pltpu.VMEM((8, tokens), F32),
            pltpu.VMEM((8, 8, tokens), F32),
            pltpu.VMEM((16, 8, 128), F32),
            pltpu.VMEM((8, 128), F32),
            pltpu.VMEM((2, 2) + block, BF16),
            pltpu.VMEM((2, 2, 2) + block, BF16),
            pltpu.VMEM((2, 2, 2, 2, part, quarter), BF16),
            pltpu.VMEM((2, 2, 2) + block, BF16),
            pltpu.VMEM((2,) + block, BF16),
            pltpu.VMEM((2,) + block, BF16),
            dma((10,)),
            dma((2, 2)), dma((2, 2)),
            dma((2,)), dma((2,)),
            dma((22,)), dma((22,)),
            dma((2, 2, 2, 2)), dma((2, 2, 2, 2)),
            dma((2, 2, 2, 2)), dma((2, 2, 2, 2)),
            dma((2, 2)), dma((2, 2)),
        ],
        compiler_params=pltpu.CompilerParams(
            collective_id=1, has_side_effects=True, vmem_limit_bytes=60 << 20
        ),
        name="attention_and_reductions",
    )(w_ref, nt_ref, nt_far_ref, q_ref, kv_ref, do_ref, lo_ref, proj_ref, q_mul_ref, k_mul_ref, x_mine_ref, inv_ref)


def gather_and_project(x_ref, wq_ref, wk_ref, wv_ref, gain_ref, q_mul_ref, k_mul_ref):
    tokens, width = x_ref.shape
    deep, q_cols = wq_ref.shape
    kv_cols = wk_ref.shape[1]
    head = q_mul_ref.shape[1]
    wing = q_cols // 2

    def kernel(x, wq, wk, wv, gain, q_mul, k_mul, w_all, nt, nt_far, proj, q16, kv, inv, x_mine, normed, one_of, xt,
               x_s, x_r, near_s, near_r, far_s, far_r, twin_s, twin_r, swap_s, swap_r, kv_s, kv_r):
        c, f = lax.axis_index("ctx"), lax.axis_index("fsdp")
        z, xl, core = c // 4, lax.rem(c // 2, 2), lax.rem(c, 2)
        twin = (z * 4 + xl * 2 + 1 - core, f)
        mate = (z * 4 + (1 - xl) * 2 + core, f)
        along = lambda k: (lax.rem(z + k, 4) * 4 + xl * 2 + core, f)
        later = [(lax.rem(c + k, 16), f) for k in (1, 2)]
        earlier = [(lax.rem(c + 16 - k, 16), f) for k in (1, 2)]

        barrier = pltpu.get_barrier_semaphore()
        for to in [twin, mate, along(1), along(3)] + later + earlier:
            pl.semaphore_signal(barrier, inc=1, device_id=to, device_id_type=MESH)
        pl.semaphore_wait(barrier, 8)

        def rows(k, xx, who=None):
            place = lax.rem(z + k, 4) * 4 + (1 - xl if xx else xl) * 2 + (core if who is None else who)
            return pl.ds(pl.multiple_of(place * deep, 16), deep)

        def copy(src, dst, ss, rs, to):
            return pltpu.make_async_remote_copy(
                src_ref=src, dst_ref=dst, send_sem=ss, recv_sem=rs, device_id=to, device_id_type=MESH
            )

        started = []

        def go(ref, ss, rs, to):
            cp = copy(ref, ref, ss, rs, to)
            cp.start()
            started.append(cp)

        def wait_for(ref, ss, rs):
            copy(ref, ref, ss, rs, twin).wait_recv()

        def to_twin(s, k, xx):
            go(w_all.at[s, rows(k, xx)], twin_s.at[s, xx, k], twin_r.at[s, xx, k], twin)

        def to_near(s, xx):
            for n, k in enumerate((1, 3)):
                go(w_all.at[s, rows(0, xx)], near_s.at[s, xx, n], near_r.at[s, xx, n], along(k))

        def near_and_forward(s, xx):
            for n, k in enumerate((3, 1)):
                wait_for(w_all.at[s, rows(k, xx)], near_s.at[s, xx, n], near_r.at[s, xx, n])
                go(w_all.at[s, rows(k, xx), pl.ds(n * wing, wing)], far_s.at[s, xx, n], far_r.at[s, xx, n],
                   along(1 if n == 0 else 3))
                to_twin(s, k, xx)

        def far(s, xx):
            for n in range(2):
                wait_for(w_all.at[s, rows(2, xx), pl.ds(n * wing, wing)], far_s.at[s, xx, n], far_r.at[s, xx, n])
            to_twin(s, 2, xx)

        def to_mate(s):
            go(w_all.at[s, rows(0, 0)], x_s.at[s], x_r.at[s], mate)

        def from_mate(s):
            wait_for(w_all.at[s, rows(0, 1)], x_s.at[s], x_r.at[s])

        def all_from_twin(s, ks):
            for xx in range(2):
                for k in ks:
                    wait_for(w_all.at[s, rows(k, xx, 1 - core)], twin_s.at[s, xx, k], twin_r.at[s, xx, k])

        w_all[1, rows(0, 0), :kv_cols] = wk[...]
        w_all[1, rows(0, 0), kv_cols:] = wv[...]
        to_mate(1)
        to_near(1, 0)
        w_all[0, rows(0, 0), :] = wq[...]
        to_twin(1, 0, 0)

        tile = 32

        def norm_tile(i, carry):
            at = pl.ds(pl.multiple_of(i * tile, tile), tile)
            wide = x[at, :].astype(F32)
            one = lax.rsqrt(jnp.sum(wide * wide, axis=1, keepdims=True) * (1.0 / width) + epsilon)
            one_of[at, :] = jnp.broadcast_to(one, (tile, 128))
            normed[at, :] = (wide * one * gain[...]).astype(BF16)
            return carry

        lax.fori_loop(0, tokens // tile, norm_tile, 0)
        from_mate(1)
        to_near(1, 1)
        to_mate(0)
        to_twin(1, 0, 1)

        strip = 256

        def turn(i, carry):
            at = pl.ds(pl.multiple_of(i * strip, strip), strip)
            nt[at, :] = normed[:, at].T
            xt[at, :] = x[:, at].T
            return carry

        near_and_forward(1, 0)
        to_near(0, 0)
        to_twin(0, 0, 0)
        lax.fori_loop(0, width // strip, turn, 0)
        inv[...] = one_of[...].T[:1]
        x_mine[...] = xt[pl.ds(pl.multiple_of(f * (2 * deep), 16), 2 * deep), :]
        near_and_forward(1, 1)
        from_mate(0)
        to_near(0, 1)
        to_twin(0, 0, 1)
        swaps = []
        for j in range(8):
            src = pl.ds(pl.multiple_of((j * 2 + 1 - core) * deep, 16), deep)
            cp = copy(nt.at[src], nt_far.at[j], swap_s.at[j], swap_r.at[j], twin)
            cp.start()
            swaps.append(cp)
        far(1, 0)
        far(1, 1)
        all_from_twin(1, range(4))
        proj[:, q_cols:] = jnp.dot(normed[...], w_all[1], preferred_element_type=F32)

        def head_norm(raw, mul):
            one = lax.rsqrt(jnp.mean(raw * raw, axis=1, keepdims=True) + epsilon)
            return (raw * one * mul).astype(BF16)

        last = pl.ds(2 * tokens, tokens)
        for g in range(kv_cols // head):
            at = slice(q_cols + g * head, q_cols + (g + 1) * head)
            kv[last, g * head : (g + 1) * head] = head_norm(proj[:, at], k_mul[...])
        kv[last, kv_cols:] = proj[:, q_cols + kv_cols :].astype(BF16)
        passed = []
        for n in range(2):
            cp = copy(kv.at[last], kv.at[pl.ds((1 - n) * tokens, tokens)], kv_s.at[n], kv_r.at[n], later[n])
            cp.start()
            passed.append(cp)
        near_and_forward(0, 0)
        near_and_forward(0, 1)
        all_from_twin(0, (0, 1, 3))
        span = width // 2
        pair = z // 2
        near_half = pl.ds(pl.multiple_of(pair * span, 128), span)
        proj[:, :q_cols] = jnp.dot(normed[:, near_half], w_all[0, near_half, :], preferred_element_type=F32)
        far(0, 0)
        far(0, 1)
        all_from_twin(0, (2,))
        far_half = pl.ds(pl.multiple_of((1 - pair) * span, 128), span)
        proj[:, :q_cols] += jnp.dot(normed[:, far_half], w_all[0, far_half, :], preferred_element_type=F32)
        for h in range(q_cols // head):
            at = slice(h * head, (h + 1) * head)
            q16[:, at] = head_norm(proj[:, at], q_mul[...])
        for cp in passed + swaps:
            cp.wait_recv()
        for cp in passed + swaps + started:
            cp.wait_send()

    vm = pl.BlockSpec(memory_space=pltpu.VMEM)
    dma = pltpu.SemaphoreType.DMA
    return pl.pallas_call(
        kernel,
        out_shape=(
            jax.ShapeDtypeStruct((2, width, q_cols), BF16),
            jax.ShapeDtypeStruct((width, tokens), BF16),
            jax.ShapeDtypeStruct((8, deep, tokens), BF16),
            jax.ShapeDtypeStruct((tokens, 2 * q_cols), F32),
            jax.ShapeDtypeStruct((tokens, q_cols), BF16),
            jax.ShapeDtypeStruct((3 * tokens, 2 * kv_cols), BF16),
            jax.ShapeDtypeStruct((1, tokens), F32),
            jax.ShapeDtypeStruct((2 * deep, tokens), BF16),
        ),
        in_specs=[vm] * 7,
        out_specs=(vm,) * 8,
        scratch_shapes=[
            pltpu.VMEM((tokens, width), BF16),
            pltpu.VMEM((tokens, 128), F32),
            pltpu.VMEM((width, tokens), BF16),
            dma((2,)), dma((2,)),
            dma((2, 2, 2)), dma((2, 2, 2)),
            dma((2, 2, 2)), dma((2, 2, 2)),
            dma((2, 2, 4)), dma((2, 2, 4)),
            dma((8,)), dma((8,)),
            dma((2,)), dma((2,)),
        ],
        compiler_params=pltpu.CompilerParams(
            collective_id=2, has_side_effects=True, vmem_limit_bytes=60 << 20
        ),
        name="gather_and_project",
    )(x_ref, wq_ref, wk_ref, wv_ref, gain_ref, q_mul_ref, k_mul_ref)


def on_device(
    inputs,
    output_cotangent,
    w_query,
    key_projection,
    value_projection,
    norm_gain,
    q_gain,
    key_norm_gain,
    half_lengths,
):
    tokens = inputs.shape[0]
    model_width = inputs.shape[1]
    head_dim = q_gain.shape[0]
    q_cols = w_query.shape[1]
    kv_cols = key_projection.shape[1]
    ctx_count = lax.axis_size("ctx")
    ctx_index = lax.axis_index("ctx")
    first_row = ctx_index * tokens
    grad_scale = float(tokens * ctx_count) ** (-0.5)
    query_multiplier = q_gain * query_scale
    gathered, normed_t, normed_far, projected, query_rows, kv_span, inv_row, inputs_mine = gather_and_project(
        inputs, w_query, key_projection, value_projection, norm_gain[None],
        (query_multiplier * LOG2E)[None], key_norm_gain[None],
    )
    fsdp_index = lax.axis_index("fsdp")
    fsdp_count = lax.axis_size("fsdp")
    features = model_width // fsdp_count
    hat_mine = inputs_mine.astype(jnp.float32) * inv_row
    gain_mine = lax.dynamic_slice_in_dim(norm_gain, fsdp_index * features, features, 0)
    halves = half_lengths.shape[0]
    upto = lax.iota(jnp.int32, halves)[None, :] <= lax.iota(jnp.int32, halves)[:, None]
    segment_ends = jnp.sum(jnp.where(upto, half_lengths[None, :], 0), axis=1)
    positions = first_row + lax.iota(jnp.int32, tokens)
    begun = jnp.max(jnp.where(segment_ends[None, :] <= positions[:, None], segment_ends[None, :], 0), axis=1)
    lowest = jnp.maximum(positions - (WIN - 1), begun) - (first_row - REACH * tokens)
    d_mine, weight_sum, sum_f, sum_c = attention_and_reductions(
        gathered, normed_t, normed_far, query_rows, kv_span, output_cotangent, lowest[:, None], projected,
        query_multiplier[None], key_norm_gain[None], inputs_mine, inv_row, grad_scale, query_scale,
    )
    d_mine = d_mine.reshape(features, tokens)
    row_dot = sum_f[0]
    upstream = d_mine * gain_mine[:, None]
    grad_inputs = (inv_row * (upstream - hat_mine * (row_dot[None, :] / model_width))).astype(jnp.bfloat16).T
    norm_row_dots = row_dot * float(model_width) ** (-0.5)
    own_features = model_width // (fsdp_count * ctx_count)
    gain_sum = lax.dynamic_slice_in_dim(
        sum_c[:6].reshape(6 * 128), ctx_index * own_features, own_features, 0
    )
    grad_q_gain, grad_k_gain = sum_c[6], sum_c[7]
    return (
        grad_inputs,
        weight_sum[:, :q_cols],
        weight_sum[:, q_cols : q_cols + kv_cols],
        weight_sum[:, q_cols + kv_cols :],
        gain_sum,
        grad_q_gain,
        grad_k_gain,
        norm_row_dots,
    )


def solution(mesh):
    placed = (
        P("ctx", None),
        P("ctx", "fsdp"),
        P("ctx", "fsdp"),
        P("ctx", "fsdp"),
        P("ctx", "fsdp"),
        P(),
        P(),
        P(),
        P(),
    )
    return jax.shard_map(
        on_device,
        mesh=mesh,
        in_specs=placed,
        out_specs=(
            P("ctx", "fsdp"),
            P("ctx", "fsdp"),
            P("ctx", "fsdp"),
            P("ctx", "fsdp"),
            P(("fsdp", "ctx")),
            P(),
            P(),
            P("ctx"),
        ),
        check_vma=False,
    )
```

profile of v0, /device:TPU:1, one launch (start us, length us, event | category | flops | bytes accessed | tf_op | source)
XLA Modules:
  0.0 190.1 jit_solution(9397248781383648435)
XLA Ops:
  0.6 0.8 select_reduce_fusion.1
  1.4 0.1 select_reduce_fusion
  1.5 0.1 copy.20
  1.7 0.8 maximum_subtract_fusion.lo
  2.4 1.2 multiply_bitcast_fusion
  3.6 1.4 broadcast_in_dim.43.gain
  5.0 84.5 %gather_and_project.1 = (bf16[2,5376,512]{2,1,0:T(8,128)(2,1)}, bf16[5376,512]{1,0:T(8,128)(2,1)}, bf16[8,336,512]{2,1,0:T(8,128)(2,1)}, f32[512,1024]{1,0:T(8,1...) custom-call(bf16[512,5376]{1,0:T(8,128)(2,1)} %x.1, ...), custom_call_target="tpu_custom_call" | custom-call | tf_op jit(solution)/shard_map/gather_and_project/pallas_call | solution.py:501
  89.5 0.0 copy-start
  89.5 0.0 copy-start.2
  89.5 93.4 %attention_and_reductions.1 = (f32[2,336,512]{2,1,0:T(8,128)}, bf16[336,1024]{1,0:T(8,128)(2,1)}, f32[8,512]{1,0:T(8,128)}, f32[8,128]{1,0:T(8,128)}) custom-call(bf16[2,5376,512]{2,1,0:T(8,128)(2,1)} %get-tuple-element.21.w_hbm, bf16[5376,512]{1,0:T(8,128)(2,1)} %get-tuple-element.22.nt_hbm, bf16[8,336,512]{2,1,0:T(8,128)(2,1)} %get-tuple-element.23.nt_far_hbm, ...), custom_call_target="tpu_custom_call" | custom-call | tf_op jit(solution)/shard_map/attention_and_reductions/pallas_call | solution.py:293
  182.9 1.3 slice_multiply_fusion
  184.2 0.8 dynamic_slice.6
  184.9 0.0 copy-done
  185.0 0.0 copy-done.2
  185.0 0.0 copy-start.1
  185.0 2.6 %fusion.2 = bf16[672,512]{1,0:T(8,128)(2,1)} fusion(f32[2,336,512]{2,1,0:T(8,128)} %get-tuple-element.28, bf16[672,512]{1,0:T(8,128)(2,1)S(1)} %copy-done, f32[512]{0:T(512)S(1)} %bitcast.27, f32[672]{0:T(1024)S(1)} %dynamic_slice.6, f32[512]{0:T(512)S(1)} %bitcast.26), kind=kLoop, calls=%fused_computation.3 | loop fusion | flops 2408448 | bytes 2759296 | tf_op jit(solution)/shard_map/convert_element_type | solution.py:576
  187.5 0.0 copy-start.3
  187.5 0.0 copy-done.1
  187.5 0.7 fusion.3
  188.3 0.8 slice.22
  189.0 0.0 copy-done.3
  189.0 0.6 dynamic_slice.7
  189.6 0.5 slice_bitcast_fusion.1
  (2 shorter events, 0.0 us)
Async XLA Ops:
  89.5 95.5 %copy-start = (bf16[672,512]{1,0:T(8,128)(2,1)S(1)}, bf16[672,512]{1,0:T(8,128)(2,1)}, u32[]{:S(2)}) copy-start(bf16[672,512]{1,0:T(8,128)(2,1)} %get-tuple-element.27.x_mine) | copy-start | bytes 2064388
  89.5 95.5 %copy-start.2 = (f32[1,512]{1,0:T(1,128)S(1)}, f32[1,512]{1,0:T(1,128)}, u32[]{:S(2)}) copy-start(f32[1,512]{1,0:T(1,128)} %get-tuple-element.20.inv) | copy-start | bytes 6148
  185.0 2.6 %copy-start.1 = (bf16[336,1024]{1,0:T(8,128)(2,1)S(1)}, bf16[336,1024]{1,0:T(8,128)(2,1)}, u32[]{:S(2)}) copy-start(bf16[336,1024]{1,0:T(8,128)(2,1)} %get-tuple-element.30) | copy-start | bytes 2064388
  187.5 1.5 copy-start.3
where the time goes:
time: 190 us
  Pallas kernels  178 us (94%)
  other arithmetic  6.65 us (4%)
  local copies, waits for them, and re-layouts  4.9 us (3%)
    pallas_call x1, Pallas kernels, attention_and_reductions(): pl.pallas_call(kernel, out_shape=(jax.ShapeDtypeStruct(block, F32), jax.S...  93.4 us
    pallas_call x1, Pallas kernels, gather_and_project(): pl.pallas_call(kernel, out_shape=(jax.ShapeDtypeStruct((2, width, q_cols)...  84.5 us

commit v1 on v0

--- a/solution.py
+++ b/solution.py
@@ -20,22 +20,23 @@
 LOG2E = 1.4426950408889634
 
 
-def attention_and_reductions(w_ref, nt_ref, nt_far_ref, q_ref, kv_ref, do_ref, lo_ref, proj_ref, q_mul_ref, k_mul_ref,
+def attention_and_reductions(w_ref, nt_ref, nt_far_ref, q_ref, kv_ref, do_ref, lengths_ref, proj_ref, q_gain_ref, k_mul_ref,
                              x_mine_ref, inv_ref, scale, q_scale):
     tokens, q_cols = q_ref.shape
     cols = proj_ref.shape[1]
     part = w_ref.shape[1] // 16
     wing = cols // 2
     kvs = kv_ref.shape[1] // 2
-    head = q_mul_ref.shape[1]
+    head = q_gain_ref.shape[1]
     kv_heads = kvs // head
+    segs = lengths_ref.shape[0]
     group = q_cols // kvs
     half = tokens // 2
     span = 5 * half
     reach = kv_ref.shape[0]
     quarter = tokens // 2
 
-    def kernel(w_hbm, nt_hbm, nt_far_hbm, q, kv, do, lo, proj, q_mul, k_mul, x_mine, inv,
+    def kernel(w_hbm, nt_hbm, nt_far_hbm, q, kv, do, lengths, proj, q_gain, k_mul, x_mine, inv,
                dn_out, wg_out, sum_f, sum_c,
                w, nt, nt_far, v_one, e_all, mask, dkey, dval, kvg, kvg_in, own_kv, d, d_far, small,
                slots_f, slots_c, mine_c, far, near, far_in, near_in, cross, cross_in,
@@ -82,10 +83,20 @@
         for g in range(kv_heads):
             v_one[g, :, :head] = kv[:, kvs + g * head : kvs + (g + 1) * head]
             v_one[g, :, head:] = ones
+        q_mul = q_gain[...] * q_scale
+        first_row = c * tokens
+        ends = [lengths[0]]
+        for n in range(1, segs):
+            ends.append(ends[-1] + lengths[n])
         for t in range(2):
+            at = lax.broadcasted_iota(jnp.int32, (half, 1), 0) + (first_row + t * half)
+            begun = jnp.zeros((half, 1), jnp.int32)
+            for end in ends:
+                begun = jnp.where(at >= end, end, begun)
+            low = jnp.maximum(at - (WIN - 1), begun) - (first_row - REACH * tokens)
             col = lax.broadcasted_iota(jnp.int32, (half, span), 1) + t * half
             row = lax.broadcasted_iota(jnp.int32, (half, span), 0) + t * half
-            seen = (col >= lo[t * half : (t + 1) * half, :]) & (col <= row + 2 * tokens)
+            seen = (col >= low) & (col <= row + 2 * tokens)
             mask[t] = jnp.where(seen, 1.0, 0.0).astype(BF16)
         lane = lax.broadcasted_iota(jnp.int32, (half, head), 1)
 
@@ -124,7 +135,7 @@
                     dq = jnp.dot(ds, keys, preferred_element_type=F32)
                     dkey[ks, :] += lax.dot_general(ds, qt, TN, preferred_element_type=F32)
                     dval[ks, :] += lax.dot_general(e_all[...], scaled16, TN, preferred_element_type=F32)
-                    d[qs, hc], term_q = norm_back(dq, proj[qs, hc], q_mul[...])
+                    d[qs, hc], term_q = norm_back(dq, proj[qs, hc], q_mul)
                     q_term += term_q
             if g == 0:
                 pl.semaphore_wait(barrier, len(partners))
@@ -192,6 +203,8 @@
         swap_q.wait_recv()
         send_far(1, 0, 0)
         make_near(1, 0, 0)
+        send_far(1, 1, 0)
+        make_near(1, 1, 0)
         send_near(1, 0, 0)
 
         k_term = jnp.zeros((1, head), F32)
@@ -211,15 +224,19 @@
         send_far(0, 0, 0)
         make_near(0, 0, 0)
         send_far(0, 0, 1)
+        send_near(1, 1, 0)
         send_near(0, 0, 0)
+        make_near(0, 0, 1)
+        send_far(0, 1, 0)
         swap_kv.wait_recv()
         send_far(1, 0, 1)
-        make_near(0, 0, 1)
-        send_far(0, 1, 0)
+        make_near(1, 0, 1)
         send_near(0, 0, 1)
-        make_near(1, 0, 1)
-        send_far(1, 1, 0)
+        send_far(1, 1, 1)
+        make_near(1, 1, 1)
+        make_near(0, 1, 0)
         send_near(1, 0, 1)
+        send_cross(1, 0)
 
         product = d[...].astype(F32) * proj[...]
         upper = product.astype(BF16)
@@ -233,20 +250,14 @@
         slots_f[f] = small[...]
         few = [go(small, slots_f.at[f], few_s.at[k], few_r.at[k], to) for k, to in enumerate(peers_f)]
 
+        send_far(0, 1, 1)
+        make_near(0, 1, 1)
+        send_near(0, 1, 0)
         send_cross(0, 0)
-        make_near(0, 1, 0)
-        send_far(0, 1, 1)
-        send_near(0, 1, 0)
-        send_cross(1, 0)
+        send_near(1, 1, 1)
         send_cross(0, 1)
-        make_near(1, 1, 0)
-        send_far(1, 1, 1)
-        send_near(1, 1, 0)
         send_cross(1, 1)
-        make_near(0, 1, 1)
         send_near(0, 1, 1)
-        make_near(1, 1, 1)
-        send_near(1, 1, 1)
         for cp in few:
             cp.wait_recv()
         total_f = slots_f[0]
@@ -298,7 +309,7 @@
             jax.ShapeDtypeStruct((8, tokens), F32),
             jax.ShapeDtypeStruct((8, 128), F32),
         ),
-        in_specs=[anywhere] * 3 + [vm] * 9,
+        in_specs=[anywhere] * 3 + [vm] * 3 + [pl.BlockSpec(memory_space=pltpu.SMEM)] + [vm] * 5,
         out_specs=(vm,) * 4,
         scratch_shapes=[
             pltpu.VMEM(w_ref.shape, BF16),
@@ -336,17 +347,18 @@
             collective_id=1, has_side_effects=True, vmem_limit_bytes=60 << 20
         ),
         name="attention_and_reductions",
-    )(w_ref, nt_ref, nt_far_ref, q_ref, kv_ref, do_ref, lo_ref, proj_ref, q_mul_ref, k_mul_ref, x_mine_ref, inv_ref)
-
-
-def gather_and_project(x_ref, wq_ref, wk_ref, wv_ref, gain_ref, q_mul_ref, k_mul_ref):
+    )(w_ref, nt_ref, nt_far_ref, q_ref, kv_ref, do_ref, lengths_ref, proj_ref, q_gain_ref, k_mul_ref, x_mine_ref, inv_ref)
+
+
+def gather_and_project(x_ref, wq_ref, wk_ref, wv_ref, gain_ref, q_gain_ref, k_mul_ref, q_scale):
     tokens, width = x_ref.shape
     deep, q_cols = wq_ref.shape
     kv_cols = wk_ref.shape[1]
-    head = q_mul_ref.shape[1]
+    head = q_gain_ref.shape[1]
     wing = q_cols // 2
 
-    def kernel(x, wq, wk, wv, gain, q_mul, k_mul, w_all, nt, nt_far, proj, q16, kv, inv, x_mine, normed, one_of, xt,
+    def kernel(x_hbm, wq, wk, wv, gain, q_gain, k_mul, w_out, nt_out, nt_far, proj, q16, kv, inv, x_mine,
+               x, w_all, nt, normed, one_of, xt, own_s,
                x_s, x_r, near_s, near_r, far_s, far_r, twin_s, twin_r, swap_s, swap_r, kv_s, kv_r):
         c, f = lax.axis_index("ctx"), lax.axis_index("fsdp")
         z, xl, core = c // 4, lax.rem(c // 2, 2), lax.rem(c, 2)
@@ -356,6 +368,8 @@
         later = [(lax.rem(c + k, 16), f) for k in (1, 2)]
         earlier = [(lax.rem(c + 16 - k, 16), f) for k in (1, 2)]
 
+        x_copy = pltpu.make_async_copy(x_hbm, x, own_s.at[0])
+        x_copy.start()
         barrier = pltpu.get_barrier_semaphore()
         for to in [twin, mate, along(1), along(3)] + later + earlier:
             pl.semaphore_signal(barrier, inc=1, device_id=to, device_id_type=MESH)
@@ -424,9 +438,13 @@
             wide = x[at, :].astype(F32)
             one = lax.rsqrt(jnp.sum(wide * wide, axis=1, keepdims=True) * (1.0 / width) + epsilon)
             one_of[at, :] = jnp.broadcast_to(one, (tile, 128))
-            normed[at, :] = (wide * one * gain[...]).astype(BF16)
+            hat = wide * one
+            for j in range(width // 128):
+                strip_j = slice(j * 128, (j + 1) * 128)
+                normed[at, strip_j] = (hat[:, strip_j] * gain[j : j + 1, :]).astype(BF16)
             return carry
 
+        x_copy.wait()
         lax.fori_loop(0, tokens // tile, norm_tile, 0)
         from_mate(1)
         to_near(1, 1)
@@ -445,6 +463,8 @@
         to_near(0, 0)
         to_twin(0, 0, 0)
         lax.fori_loop(0, width // strip, turn, 0)
+        outward = [pltpu.make_async_copy(nt, nt_out, own_s.at[1])]
+        outward[0].start()
         inv[...] = one_of[...].T[:1]
         x_mine[...] = xt[pl.ds(pl.multiple_of(f * (2 * deep), 16), 2 * deep), :]
         near_and_forward(1, 1)
@@ -460,6 +480,12 @@
         far(1, 0)
         far(1, 1)
         all_from_twin(1, range(4))
+        def to_hbm(s, at, n):
+            cp = pltpu.make_async_copy(w_all.at[s, at], w_out.at[s, at], own_s.at[n])
+            cp.start()
+            outward.append(cp)
+
+        to_hbm(1, pl.ds(0, width), 2)
         proj[:, q_cols:] = jnp.dot(normed[...], w_all[1], preferred_element_type=F32)
 
         def head_norm(raw, mul):
@@ -482,21 +508,26 @@
         span = width // 2
         pair = z // 2
         near_half = pl.ds(pl.multiple_of(pair * span, 128), span)
+        to_hbm(0, near_half, 3)
         proj[:, :q_cols] = jnp.dot(normed[:, near_half], w_all[0, near_half, :], preferred_element_type=F32)
         far(0, 0)
         far(0, 1)
         all_from_twin(0, (2,))
         far_half = pl.ds(pl.multiple_of((1 - pair) * span, 128), span)
+        to_hbm(0, far_half, 4)
         proj[:, :q_cols] += jnp.dot(normed[:, far_half], w_all[0, far_half, :], preferred_element_type=F32)
         for h in range(q_cols // head):
             at = slice(h * head, (h + 1) * head)
-            q16[:, at] = head_norm(proj[:, at], q_mul[...])
+            q16[:, at] = head_norm(proj[:, at], q_gain[...] * (q_scale * LOG2E))
         for cp in passed + swaps:
             cp.wait_recv()
         for cp in passed + swaps + started:
             cp.wait_send()
+        for cp in outward:
+            cp.wait()
 
     vm = pl.BlockSpec(memory_space=pltpu.VMEM)
+    anywhere = pl.BlockSpec(memory_space=pl.ANY)
     dma = pltpu.SemaphoreType.DMA
     return pl.pallas_call(
         kernel,
@@ -510,12 +541,16 @@
             jax.ShapeDtypeStruct((1, tokens), F32),
             jax.ShapeDtypeStruct((2 * deep, tokens), BF16),
         ),
-        in_specs=[vm] * 7,
-        out_specs=(vm,) * 8,
+        in_specs=[anywhere] + [vm] * 6,
+        out_specs=(anywhere,) * 3 + (vm,) * 5,
         scratch_shapes=[
+            pltpu.VMEM((tokens, width), BF16),
+            pltpu.VMEM((2, width, q_cols), BF16),
+            pltpu.VMEM((width, tokens), BF16),
             pltpu.VMEM((tokens, width), BF16),
             pltpu.VMEM((tokens, 128), F32),
             pltpu.VMEM((width, tokens), BF16),
+            dma((5,)),
             dma((2,)), dma((2,)),
             dma((2, 2, 2)), dma((2, 2, 2)),
             dma((2, 2, 2)), dma((2, 2, 2)),
@@ -527,7 +562,7 @@
             collective_id=2, has_side_effects=True, vmem_limit_bytes=60 << 20
         ),
         name="gather_and_project",
-    )(x_ref, wq_ref, wk_ref, wv_ref, gain_ref, q_mul_ref, k_mul_ref)
+    )(x_ref, wq_ref, wk_ref, wv_ref, gain_ref, q_gain_ref, k_mul_ref)
 
 
 def on_device(
@@ -548,27 +583,19 @@
     kv_cols = key_projection.shape[1]
     ctx_count = lax.axis_size("ctx")
     ctx_index = lax.axis_index("ctx")
-    first_row = ctx_index * tokens
     grad_scale = float(tokens * ctx_count) ** (-0.5)
-    query_multiplier = q_gain * query_scale
     gathered, normed_t, normed_far, projected, query_rows, kv_span, inv_row, inputs_mine = gather_and_project(
-        inputs, w_query, key_projection, value_projection, norm_gain[None],
-        (query_multiplier * LOG2E)[None], key_norm_gain[None],
+        inputs, w_query, key_projection, value_projection, norm_gain.reshape(model_width // 128, 128),
+        q_gain[None], key_norm_gain[None], query_scale,
     )
     fsdp_index = lax.axis_index("fsdp")
     fsdp_count = lax.axis_size("fsdp")
     features = model_width // fsdp_count
     hat_mine = inputs_mine.astype(jnp.float32) * inv_row
     gain_mine = lax.dynamic_slice_in_dim(norm_gain, fsdp_index * features, features, 0)
-    halves = half_lengths.shape[0]
-    upto = lax.iota(jnp.int32, halves)[None, :] <= lax.iota(jnp.int32, halves)[:, None]
-    segment_ends = jnp.sum(jnp.where(upto, half_lengths[None, :], 0), axis=1)
-    positions = first_row + lax.iota(jnp.int32, tokens)
-    begun = jnp.max(jnp.where(segment_ends[None, :] <= positions[:, None], segment_ends[None, :], 0), axis=1)
-    lowest = jnp.maximum(positions - (WIN - 1), begun) - (first_row - REACH * tokens)
     d_mine, weight_sum, sum_f, sum_c = attention_and_reductions(
-        gathered, normed_t, normed_far, query_rows, kv_span, output_cotangent, lowest[:, None], projected,
-        query_multiplier[None], key_norm_gain[None], inputs_mine, inv_row, grad_scale, query_scale,
+        gathered, normed_t, normed_far, query_rows, kv_span, output_cotangent, half_lengths, projected,
+        q_gain[None], key_norm_gain[None], inputs_mine, inv_row, grad_scale, query_scale,
     )
     d_mine = d_mine.reshape(features, tokens)
     row_dot = sum_f[0]

time: 190 us -> 181 us (0.953)
  Pallas kernels: 178 us -> 173 us
  other arithmetic: 6.65 us -> 3.86 us
    pallas_call x1, Pallas kernels: 84.5 us -> 77.1 us  [gather_and_project(): pl.pallas_call(kernel, out_shape=(jax.ShapeDtypeStruct((2, width, q_cols)...]
    pallas_call x1, Pallas kernels: 93.4 us -> 95.9 us  [attention_and_reductions(): pl.pallas_call(kernel, out_shape=(jax.ShapeDtypeStruct(block, F32), jax.S...]
where the time goes in v1:
time: 181 us
  Pallas kernels  173 us (96%)
  other arithmetic  3.86 us (2%)
  local copies, waits for them, and re-layouts  3.39 us (2%)
    pallas_call x1, Pallas kernels, attention_and_reductions(): pl.pallas_call(kernel, out_shape=(jax.ShapeDtypeStruct(block, F32), jax.S...  95.9 us
    pallas_call x1, Pallas kernels, gather_and_project(): pl.pallas_call(kernel, out_shape=(jax.ShapeDtypeStruct((2, width, q_cols)...  77.1 us

profile of v1, /device:TPU:1, one launch (start us, length us, event | category | flops | bytes accessed | tf_op | source)
XLA Modules:
  0.0 180.9 jit_solution(17620862917487511616)
XLA Ops:
  0.6 77.1 %gather_and_project.1 = (bf16[2,5376,512]{2,1,0:T(8,128)(2,1)}, bf16[5376,512]{1,0:T(8,128)(2,1)}, bf16[8,336,512]{2,1,0:T(8,128)(2,1)}, f32[512,1024]{1,0:T(8,1...) custom-call(bf16[512,5376]{1,0:T(8,128)(2,1)} %x_hbm.1, ...), custom_call_target="tpu_custom_call" | custom-call | tf_op jit(solution)/shard_map/gather_and_project/pallas_call | solution.py:532
  77.7 0.0 copy-start
  77.8 0.0 copy-start.2
  77.8 95.9 %attention_and_reductions.1 = (f32[2,336,512]{2,1,0:T(8,128)}, bf16[336,1024]{1,0:T(8,128)(2,1)}, f32[8,512]{1,0:T(8,128)}, f32[8,128]{1,0:T(8,128)}) custom-call(bf16[2,5376,512]{2,1,0:T(8,128)(2,1)} %get-tuple-element.21.w_hbm, bf16[5376,512]{1,0:T(8,128)(2,1)} %get-tuple-element.22.nt_hbm, bf16[8,336,512]{2,1,0:T(8,128)(2,1)} %get-tuple-element.23.nt_far_hbm, ...), custom_call_target="tpu_custom_call" | custom-call | tf_op jit(solution)/shard_map/attention_and_reductions/pallas_call | solution.py:304
  173.6 1.3 slice_multiply_fusion
  174.9 0.8 dynamic_slice.6
  175.7 0.0 copy-done
  175.7 0.0 copy-done.2
  175.7 0.0 copy-start.1
  175.7 2.6 %fusion.2 = bf16[672,512]{1,0:T(8,128)(2,1)} fusion(f32[2,336,512]{2,1,0:T(8,128)} %get-tuple-element.28, bf16[672,512]{1,0:T(8,128)(2,1)S(1)} %copy-done, f32[512]{0:T(512)S(1)} %bitcast.24, f32[672]{0:T(1024)S(1)} %dynamic_slice.6, f32[512]{0:T(512)S(1)} %bitcast.23), kind=kLoop, calls=%fused_computation.3 | loop fusion | flops 2408448 | bytes 2759296 | tf_op jit(solution)/shard_map/convert_element_type | solution.py:603
  178.3 0.0 copy-start.3
  178.3 0.0 copy-done.1
  178.3 0.7 fusion.3
  179.0 0.8 slice.22
  179.8 0.0 copy-done.3
  179.8 0.6 dynamic_slice.7
  180.4 0.5 slice_bitcast_fusion.1
  (1 shorter events, 0.0 us)
Async XLA Ops:
  77.7 98.0 %copy-start = (bf16[672,512]{1,0:T(8,128)(2,1)S(1)}, bf16[672,512]{1,0:T(8,128)(2,1)}, u32[]{:S(2)}) copy-start(bf16[672,512]{1,0:T(8,128)(2,1)} %get-tuple-element.27.x_mine) | copy-start | bytes 2064388
  77.8 98.0 %copy-start.2 = (f32[1,512]{1,0:T(1,128)S(1)}, f32[1,512]{1,0:T(1,128)}, u32[]{:S(2)}) copy-start(f32[1,512]{1,0:T(1,128)} %get-tuple-element.20.inv) | copy-start | bytes 6148
  175.7 2.6 %copy-start.1 = (bf16[336,1024]{1,0:T(8,128)(2,1)S(1)}, bf16[336,1024]{1,0:T(8,128)(2,1)}, u32[]{:S(2)}) copy-start(bf16[336,1024]{1,0:T(8,128)(2,1)} %get-tuple-element.30) | copy-start | bytes 2064388
  178.3 1.5 copy-start.3

commit v2 on v1

--- a/solution.py
+++ b/solution.py
@@ -204,8 +204,8 @@
         send_far(1, 0, 0)
         make_near(1, 0, 0)
         send_far(1, 1, 0)
+        send_near(1, 0, 0)
         make_near(1, 1, 0)
-        send_near(1, 0, 0)
 
         k_term = jnp.zeros((1, head), F32)
         for cp in kv_copies:
@@ -224,19 +224,18 @@
         send_far(0, 0, 0)
         make_near(0, 0, 0)
         send_far(0, 0, 1)
-        send_near(1, 1, 0)
-        send_near(0, 0, 0)
-        make_near(0, 0, 1)
-        send_far(0, 1, 0)
         swap_kv.wait_recv()
         send_far(1, 0, 1)
+        send_near(0, 0, 0)
         make_near(1, 0, 1)
+        make_near(0, 0, 1)
+        send_cross(1, 0)
+        send_far(0, 1, 0)
         send_near(0, 0, 1)
+        send_near(1, 0, 1)
+        send_near(1, 1, 0)
         send_far(1, 1, 1)
-        make_near(1, 1, 1)
         make_near(0, 1, 0)
-        send_near(1, 0, 1)
-        send_cross(1, 0)
 
         product = d[...].astype(F32) * proj[...]
         upper = product.astype(BF16)
@@ -250,13 +249,14 @@
         slots_f[f] = small[...]
         few = [go(small, slots_f.at[f], few_s.at[k], few_r.at[k], to) for k, to in enumerate(peers_f)]
 
+        send_cross(0, 0)
         send_far(0, 1, 1)
+        send_near(0, 1, 0)
+        make_near(1, 1, 1)
+        send_cross(1, 1)
         make_near(0, 1, 1)
-        send_near(0, 1, 0)
-        send_cross(0, 0)
         send_near(1, 1, 1)
         send_cross(0, 1)
-        send_cross(1, 1)
         send_near(0, 1, 1)
         for cp in few:
             cp.wait_recv()
@@ -266,12 +266,15 @@
         sum_f[...] = total_f
         for h in range(2):
             dn_out[h] = term(0, 1, 0, h)
-        for h in range(2):
+        spread = jnp.zeros((128, 128), F32)
+
+        def finish_weights(h):
             own_kv[:part, :] = term(1, 1, 0, h)
             crossed[1, h].wait_recv()
             total = own_kv[:part, :] + cross_in[1, h].astype(F32) + arrived(1, 1, h)
             wg_out[:, h * wing : (h + 1) * wing] = total.astype(BF16)
-        spread = jnp.zeros((128, 128), F32)
+
+        finish_weights(0)
         for h in range(2):
             crossed[0, h].wait_recv()
             total = dn_out[h] + cross_in[0, h].astype(F32) + arrived(0, 1, h)
@@ -288,6 +291,7 @@
         mine_c[7:8, :] = total_f[1:2, head : 2 * head]
         slots_c[c] = mine_c[...]
         few_c = [go(mine_c, slots_c.at[c], few_s.at[7 + k], few_r.at[7 + k], to) for k, to in enumerate(peers_c)]
+        finish_weights(1)
         for cp in few_c:
             cp.wait_recv()
         total_c = slots_c[0]

time: 181 us -> 176 us (0.972)
  Pallas kernels: 173 us -> 168 us
    pallas_call x1, Pallas kernels: 95.9 us -> 91.2 us  [attention_and_reductions(): pl.pallas_call(kernel, out_shape=(jax.ShapeDtypeStruct(block, F32), jax.S...]
where the time goes in v2:
time: 176 us
  Pallas kernels  168 us (95%)
  other arithmetic  3.86 us (2%)
  local copies, waits for them, and re-layouts  3.39 us (2%)
    pallas_call x1, Pallas kernels, attention_and_reductions(): pl.pallas_call(kernel, out_shape=(jax.ShapeDtypeStruct(block, F32), jax.S...  91.2 us
    pallas_call x1, Pallas kernels, gather_and_project(): pl.pallas_call(kernel, out_shape=(jax.ShapeDtypeStruct((2, width, q_cols)...  77.1 us

profile of v2, /device:TPU:1, one launch (start us, length us, event | category | flops | bytes accessed | tf_op | source)
XLA Modules:
  0.0 176.2 jit_solution(13632359363596190910)
XLA Ops:
  0.6 77.1 %gather_and_project.1 = (bf16[2,5376,512]{2,1,0:T(8,128)(2,1)}, bf16[5376,512]{1,0:T(8,128)(2,1)}, bf16[8,336,512]{2,1,0:T(8,128)(2,1)}, f32[512,1024]{1,0:T(8,1...) custom-call(bf16[512,5376]{1,0:T(8,128)(2,1)} %x_hbm.1, ...), custom_call_target="tpu_custom_call" | custom-call | tf_op jit(solution)/shard_map/gather_and_project/pallas_call | solution.py:536
  77.7 0.0 copy-start
  77.8 0.0 copy-start.2
  77.8 91.2 %attention_and_reductions.1 = (f32[2,336,512]{2,1,0:T(8,128)}, bf16[336,1024]{1,0:T(8,128)(2,1)}, f32[8,512]{1,0:T(8,128)}, f32[8,128]{1,0:T(8,128)}) custom-call(bf16[2,5376,512]{2,1,0:T(8,128)(2,1)} %get-tuple-element.21.w_hbm, bf16[5376,512]{1,0:T(8,128)(2,1)} %get-tuple-element.22.nt_hbm, bf16[8,336,512]{2,1,0:T(8,128)(2,1)} %get-tuple-element.23.nt_far_hbm, ...), custom_call_target="tpu_custom_call" | custom-call | tf_op jit(solution)/shard_map/attention_and_reductions/pallas_call | solution.py:308
  169.0 1.3 slice_multiply_fusion
  170.3 0.8 dynamic_slice.6
  171.0 0.0 copy-done
  171.0 0.0 copy-done.2
  171.0 0.0 copy-start.1
  171.0 2.6 %fusion.2 = bf16[672,512]{1,0:T(8,128)(2,1)} fusion(f32[2,336,512]{2,1,0:T(8,128)} %get-tuple-element.28, bf16[672,512]{1,0:T(8,128)(2,1)S(1)} %copy-done, f32[512]{0:T(512)S(1)} %bitcast.24, f32[672]{0:T(1024)S(1)} %dynamic_slice.6, f32[512]{0:T(512)S(1)} %bitcast.23), kind=kLoop, calls=%fused_computation.3 | loop fusion | flops 2408448 | bytes 2759296 | tf_op jit(solution)/shard_map/convert_element_type | solution.py:607
  173.6 0.0 copy-start.3
  173.6 0.0 copy-done.1
  173.6 0.7 fusion.3
  174.3 0.8 slice.22
  175.1 0.0 copy-done.3
  175.1 0.6 dynamic_slice.7
  175.7 0.5 slice_bitcast_fusion.1
  (1 shorter events, 0.0 us)
Async XLA Ops:
  77.7 93.3 %copy-start = (bf16[672,512]{1,0:T(8,128)(2,1)S(1)}, bf16[672,512]{1,0:T(8,128)(2,1)}, u32[]{:S(2)}) copy-start(bf16[672,512]{1,0:T(8,128)(2,1)} %get-tuple-element.27.x_mine) | copy-start | bytes 2064388
  77.8 93.3 %copy-start.2 = (f32[1,512]{1,0:T(1,128)S(1)}, f32[1,512]{1,0:T(1,128)}, u32[]{:S(2)}) copy-start(f32[1,512]{1,0:T(1,128)} %get-tuple-element.20.inv) | copy-start | bytes 6148
  171.0 2.6 %copy-start.1 = (bf16[336,1024]{1,0:T(8,128)(2,1)S(1)}, bf16[336,1024]{1,0:T(8,128)(2,1)}, u32[]{:S(2)}) copy-start(bf16[336,1024]{1,0:T(8,128)(2,1)} %get-tuple-element.30) | copy-start | bytes 2064388
  173.6 1.5 copy-start.3

commit v3 on v2

--- a/solution.py
+++ b/solution.py
@@ -36,9 +36,9 @@
     reach = kv_ref.shape[0]
     quarter = tokens // 2
 
-    def kernel(w_hbm, nt_hbm, nt_far_hbm, q, kv, do, lengths, proj, q_gain, k_mul, x_mine, inv,
+    def kernel(w_hbm, nt_hbm, nt_far_hbm, q, kv, do, lengths, proj_hbm, q_gain, k_mul, x_mine_hbm, inv,
                dn_out, wg_out, sum_f, sum_c,
-               w, nt, nt_far, v_one, e_all, mask, dkey, dval, kvg, kvg_in, own_kv, d, d_far, small,
+               w, nt, nt_far, proj, x_mine, v_one, e_all, mask, dkey, dval, kvg, kvg_in, own_kv, d, d_far, small,
                slots_f, slots_c, mine_c, far, near, far_in, near_in, cross, cross_in,
                fetch_sem, kvg_s, kvg_r, swap_s, swap_r, few_s, few_r, far_s, far_r, near_s, near_r, cross_s, cross_r):
         c, f = lax.axis_index("ctx"), lax.axis_index("fsdp")
@@ -63,7 +63,9 @@
         fetches = [pltpu.make_async_copy(nt_hbm.at[rows_of(j * 2 + core)], nt.at[j], fetch_sem.at[j]) for j in range(8)]
         fetches.append(pltpu.make_async_copy(nt_far_hbm, nt_far, fetch_sem.at[8]))
         fetches.append(pltpu.make_async_copy(w_hbm, w, fetch_sem.at[9]))
-        for cp in fetches:
+        fetches.append(pltpu.make_async_copy(x_mine_hbm, x_mine, fetch_sem.at[10]))
+        proj_copy = pltpu.make_async_copy(proj_hbm, proj, fetch_sem.at[11])
+        for cp in [proj_copy, *fetches]:
             cp.start()
 
         def copy(src, dst, ss, rs, to):
@@ -107,12 +109,24 @@
             back = one * (up - hat * jnp.mean(up * hat, axis=1, keepdims=True))
             return back.astype(BF16), jnp.sum(grad * hat, axis=0, keepdims=True)
 
+        proj_copy.wait()
         q_term = jnp.zeros((1, head), F32)
-        kv_copies = []
+        kv_first, kv_second = [], []
+
+        def pass_on(g):
+            kv_first[g].wait_recv()
+            pre = jnp.where(core == 1, kvg_in[g, 0].astype(F32), 0.0)
+            kvg[g, 1] = (kvg[g, 1].astype(F32) + pre).astype(BF16)
+            kv_second.append(
+                go(kvg.at[g, 1], kvg_in.at[g, 1], kvg_s.at[g, 1], kvg_r.at[g, 1], (lax.rem(c + 14, 16), f))
+            )
+
         for g in range(kv_heads):
             dkey[...] = jnp.zeros_like(dkey)
             dval[...] = jnp.zeros_like(dval)
             for r in range(group):
+                if g and r == 1:
+                    pass_on(g - 1)
                 h = g * group + r
                 hc = slice(h * head, (h + 1) * head)
                 for t in range(2):
@@ -143,12 +157,12 @@
                 away = slice((1 - n) * tokens, (2 - n) * tokens)
                 kvg[g, n, :, :head] = (dkey[away, :] * (1.0 / LOG2E)).astype(BF16)
                 kvg[g, n, :, head:] = dval[away, :].astype(BF16)
-                kv_copies.append(
-                    go(kvg.at[g, n], kvg_in.at[g, n], kvg_s.at[g, n], kvg_r.at[g, n], (lax.rem(c + 15 - n, 16), f))
-                )
+            kv_first.append(go(kvg.at[g, 0], kvg_in.at[g, 0], kvg_s.at[g, 0], kvg_r.at[g, 0], twin))
             own_kv[:, g * head : (g + 1) * head] = dkey[2 * tokens :, :] * (1.0 / LOG2E)
             own_kv[:, kvs + g * head : kvs + (g + 1) * head] = dval[2 * tokens :, :]
         swap_q = go(d.at[:, pl.ds(0, wing)], d_far.at[:, pl.ds(0, wing)], swap_s.at[0], swap_r.at[0], twin)
+
+        pass_on(kv_heads - 1)
 
         def term(m, s, k, h):
             if m == 0:
@@ -208,19 +222,20 @@
         make_near(1, 1, 0)
 
         k_term = jnp.zeros((1, head), F32)
-        for cp in kv_copies:
+        for cp in kv_second:
             cp.wait_recv()
         for g in range(kv_heads):
             at = slice(g * head, (g + 1) * head)
             there = slice(wing + g * head, wing + (g + 1) * head)
-            grad = own_kv[:, at] + (kvg_in[g, 0, :, :head].astype(F32) + kvg_in[g, 1, :, :head].astype(F32))
+            grad = own_kv[:, at] + (jnp.where(core == 0, kvg_in[g, 0, :, :head].astype(F32), 0.0) + kvg_in[g, 1, :, :head].astype(F32))
             d[:, there], term_k = norm_back(grad, proj[:, there], k_mul[...])
             k_term += term_k
             at = slice(kvs + g * head, kvs + (g + 1) * head)
-            grad = own_kv[:, at] + (kvg_in[g, 0, :, head:].astype(F32) + kvg_in[g, 1, :, head:].astype(F32))
+            grad = own_kv[:, at] + (jnp.where(core == 0, kvg_in[g, 0, :, head:].astype(F32), 0.0) + kvg_in[g, 1, :, head:].astype(F32))
             d[:, wing + kvs + g * head : wing + kvs + (g + 1) * head] = grad.astype(BF16)
         swap_kv = go(d.at[:, pl.ds(wing, wing)], d_far.at[:, pl.ds(wing, wing)], swap_s.at[1], swap_r.at[1], twin)
         fetches[9].wait()
+        fetches[10].wait()
         send_far(0, 0, 0)
         make_near(0, 0, 0)
         send_far(0, 0, 1)
@@ -243,9 +258,11 @@
         ones_row = jnp.ones((8, cols), BF16)
         dots = lax.dot_general(ones_row, upper, NT, preferred_element_type=F32)
         dots += lax.dot_general(ones_row, lower, NT, preferred_element_type=F32)
-        small[...] = dots
-        small[1:2, :head] = q_term * (scale * q_scale)
-        small[1:2, head : 2 * head] = k_term * scale
+        small[...] = jnp.zeros_like(small)
+        for n in range(tokens // 128):
+            small[n : n + 1, :] = dots[:1, n * 128 : (n + 1) * 128]
+        small[4:5, :] = q_term * (scale * q_scale)
+        small[5:6, :] = k_term * scale
         slots_f[f] = small[...]
         few = [go(small, slots_f.at[f], few_s.at[k], few_r.at[k], to) for k, to in enumerate(peers_f)]
 
@@ -276,6 +293,9 @@
 
         finish_weights(0)
         for h in range(2):
+            if h == 1:
+                for cp in sent:
+                    cp.wait_send()
             crossed[0, h].wait_recv()
             total = dn_out[h] + cross_in[0, h].astype(F32) + arrived(0, 1, h)
             dn_out[h] = total
@@ -287,8 +307,7 @@
             to_lane = jnp.where(lax.rem(at, 128) == lanes, 1.0, 0.0)
             spread += lax.dot_general(to_row.astype(BF16), to_lane.astype(BF16), TN, preferred_element_type=F32)
         mine_c[...] = spread[:8]
-        mine_c[6:7, :] = total_f[1:2, :head]
-        mine_c[7:8, :] = total_f[1:2, head : 2 * head]
+        mine_c[6:8, :] = total_f[4:6, :]
         slots_c[c] = mine_c[...]
         few_c = [go(mine_c, slots_c.at[c], few_s.at[7 + k], few_r.at[7 + k], to) for k, to in enumerate(peers_c)]
         finish_weights(1)
@@ -298,7 +317,7 @@
         for k in range(1, 16):
             total_c = total_c + slots_c[k]
         sum_c[...] = total_c
-        for cp in sent:
+        for cp in few_c:
             cp.wait_send()
 
     vm = pl.BlockSpec(memory_space=pltpu.VMEM)
@@ -310,15 +329,17 @@
         out_shape=(
             jax.ShapeDtypeStruct(block, F32),
             jax.ShapeDtypeStruct((part, cols), BF16),
-            jax.ShapeDtypeStruct((8, tokens), F32),
+            jax.ShapeDtypeStruct((8, 128), F32),
             jax.ShapeDtypeStruct((8, 128), F32),
         ),
-        in_specs=[anywhere] * 3 + [vm] * 3 + [pl.BlockSpec(memory_space=pltpu.SMEM)] + [vm] * 5,
+        in_specs=[anywhere] * 3 + [vm] * 3 + [pl.BlockSpec(memory_space=pltpu.SMEM), anywhere, vm, vm, anywhere, vm],
         out_specs=(vm,) * 4,
         scratch_shapes=[
             pltpu.VMEM(w_ref.shape, BF16),
             pltpu.VMEM((8, part, tokens), BF16),
             pltpu.VMEM((8, part, tokens), BF16),
+            pltpu.VMEM(proj_ref.shape, F32),
+            pltpu.VMEM(x_mine_ref.shape, BF16),
             pltpu.VMEM((kv_heads, reach, 2 * head), BF16),
             pltpu.VMEM((half, span), BF16),
             pltpu.VMEM((2, half, span), BF16),
@@ -329,8 +350,8 @@
             pltpu.VMEM((tokens, 2 * kvs), F32),
             pltpu.VMEM((tokens, cols), BF16),
             pltpu.VMEM((tokens, cols), BF16),
-            pltpu.VMEM((8, tokens), F32),
-            pltpu.VMEM((8, 8, tokens), F32),
+            pltpu.VMEM((8, 128), F32),
+            pltpu.VMEM((8, 8, 128), F32),
             pltpu.VMEM((16, 8, 128), F32),
             pltpu.VMEM((8, 128), F32),
             pltpu.VMEM((2, 2) + block, BF16),
@@ -339,7 +360,7 @@
             pltpu.VMEM((2, 2, 2) + block, BF16),
             pltpu.VMEM((2,) + block, BF16),
             pltpu.VMEM((2,) + block, BF16),
-            dma((10,)),
+            dma((12,)),
             dma((2, 2)), dma((2, 2)),
             dma((2,)), dma((2,)),
             dma((22,)), dma((22,)),
@@ -602,7 +623,7 @@
         q_gain[None], key_norm_gain[None], inputs_mine, inv_row, grad_scale, query_scale,
     )
     d_mine = d_mine.reshape(features, tokens)
-    row_dot = sum_f[0]
+    row_dot = sum_f[:4].reshape(tokens)
     upstream = d_mine * gain_mine[:, None]
     grad_inputs = (inv_row * (upstream - hat_mine * (row_dot[None, :] / model_width))).astype(jnp.bfloat16).T
     norm_row_dots = row_dot * float(model_width) ** (-0.5)

time: 176 us -> 174 us (0.989)
  Pallas kernels: 168 us -> 165 us
    pallas_call x1, Pallas kernels: 91.2 us -> 88.3 us  [attention_and_reductions(): pl.pallas_call(kernel, out_shape=(jax.ShapeDtypeStruct(block, F32), jax.S...]
where the time goes in v3:
time: 174 us; the launch traced here: 173 us
  Pallas kernels  165 us (95%)
  other arithmetic  3.82 us (2%)
  local copies, waits for them, and re-layouts  3.39 us (2%)
    pallas_call x1, Pallas kernels, attention_and_reductions(): pl.pallas_call(kernel, out_shape=(jax.ShapeDtypeStruct(block, F32), jax.S...  88.3 us
    pallas_call x1, Pallas kernels, gather_and_project(): pl.pallas_call(kernel, out_shape=(jax.ShapeDtypeStruct((2, width, q_cols)...  77.1 us

profile of v3, /device:TPU:1, one launch (start us, length us, event | category | flops | bytes accessed | tf_op | source)
XLA Modules:
  0.0 173.3 jit_solution(9532242607696865830)
XLA Ops:
  0.6 77.1 %gather_and_project.1 = (bf16[2,5376,512]{2,1,0:T(8,128)(2,1)}, bf16[5376,512]{1,0:T(8,128)(2,1)}, bf16[8,336,512]{2,1,0:T(8,128)(2,1)}, f32[512,1024]{1,0:T(8,1...) custom-call(bf16[512,5376]{1,0:T(8,128)(2,1)} %x_hbm.1, ...), custom_call_target="tpu_custom_call" | custom-call | tf_op jit(solution)/shard_map/gather_and_project/pallas_call | solution.py:557
  77.7 0.0 copy-start
  77.8 0.0 copy-start.2
  77.8 88.3 %attention_and_reductions.1 = (f32[2,336,512]{2,1,0:T(8,128)}, bf16[336,1024]{1,0:T(8,128)(2,1)}, f32[8,128]{1,0:T(8,128)}, f32[8,128]{1,0:T(8,128)}) custom-call(bf16[2,5376,512]{2,1,0:T(8,128)(2,1)} %get-tuple-element.21.w_hbm, bf16[5376,512]{1,0:T(8,128)(2,1)} %get-tuple-element.22.nt_hbm, bf16[8,336,512]{2,1,0:T(8,128)(2,1)} %get-tuple-element.23.nt_far_hbm, ...), custom_call_target="tpu_custom_call" | custom-call | tf_op jit(solution)/shard_map/attention_and_reductions/pallas_call | solution.py:327
  166.1 1.3 multiply_bitcast_fusion
  167.3 0.8 dynamic_slice.6
  168.1 0.0 copy-done
  168.1 0.0 copy-done.2
  168.1 0.0 copy-start.1
  168.1 2.6 %fusion.2 = bf16[672,512]{1,0:T(8,128)(2,1)} fusion(f32[2,336,512]{2,1,0:T(8,128)} %get-tuple-element.28, bf16[672,512]{1,0:T(8,128)(2,1)S(1)} %copy-done, f32[512]{0:T(512)S(1)} %get-tuple-element.35, f32[672]{0:T(1024)S(1)} %dynamic_slice.6, f32[512]{0:T(512)S(1)} %bitcast.25), kind=kLoop, calls=%fused_computation.3 | loop fusion | flops 2408448 | bytes 2759296 | tf_op jit(solution)/shard_map/convert_element_type | solution.py:628
  170.7 0.0 copy-start.3
  170.7 0.0 copy-done.1
  170.7 0.7 fusion.3
  171.4 0.8 slice.22
  172.2 0.0 copy-done.3
  172.2 0.6 dynamic_slice.7
  172.8 0.5 slice_bitcast_fusion.1
  (1 shorter events, 0.0 us)
Async XLA Ops:
  77.7 90.4 %copy-start = (bf16[672,512]{1,0:T(8,128)(2,1)S(1)}, bf16[672,512]{1,0:T(8,128)(2,1)}, u32[]{:S(2)}) copy-start(bf16[672,512]{1,0:T(8,128)(2,1)} %get-tuple-element.27.x_mine_hbm) | copy-start | bytes 2064388
  77.8 90.4 %copy-start.2 = (f32[1,512]{1,0:T(1,128)S(1)}, f32[1,512]{1,0:T(1,128)}, u32[]{:S(2)}) copy-start(f32[1,512]{1,0:T(1,128)} %get-tuple-element.20.inv) | copy-start | bytes 6148
  168.1 2.6 %copy-start.1 = (bf16[336,1024]{1,0:T(8,128)(2,1)S(1)}, bf16[336,1024]{1,0:T(8,128)(2,1)}, u32[]{:S(2)}) copy-start(bf16[336,1024]{1,0:T(8,128)(2,1)} %get-tuple-element.30) | copy-start | bytes 2064388
  170.7 1.5 copy-start.3

commit v4 on v3

--- a/solution.py
+++ b/solution.py
@@ -485,17 +485,15 @@
             return carry
 
         near_and_forward(1, 0)
-        to_near(0, 0)
-        to_twin(0, 0, 0)
         lax.fori_loop(0, width // strip, turn, 0)
         outward = [pltpu.make_async_copy(nt, nt_out, own_s.at[1])]
         outward[0].start()
         inv[...] = one_of[...].T[:1]
         x_mine[...] = xt[pl.ds(pl.multiple_of(f * (2 * deep), 16), 2 * deep), :]
         near_and_forward(1, 1)
+        to_near(0, 0)
+        to_twin(0, 0, 0)
         from_mate(0)
-        to_near(0, 1)
-        to_twin(0, 0, 1)
         swaps = []
         for j in range(8):
             src = pl.ds(pl.multiple_of((j * 2 + 1 - core) * deep, 16), deep)
@@ -503,6 +501,8 @@
             cp.start()
             swaps.append(cp)
         far(1, 0)
+        to_near(0, 1)
+        to_twin(0, 0, 1)
         far(1, 1)
         all_from_twin(1, range(4))
         def to_hbm(s, at, n):

time: 174 us -> 173 us (level)
  no operation moved by 1% of the time
where the time goes in v4:
time: 173 us
  Pallas kernels  165 us (95%)
  other arithmetic  3.82 us (2%)
  local copies, waits for them, and re-layouts  3.39 us (2%)
    pallas_call x1, Pallas kernels, attention_and_reductions(): pl.pallas_call(kernel, out_shape=(jax.ShapeDtypeStruct(block, F32), jax.S...  87.7 us
    pallas_call x1, Pallas kernels, gather_and_project(): pl.pallas_call(kernel, out_shape=(jax.ShapeDtypeStruct((2, width, q_cols)...  77.1 us

profile of v4, /device:TPU:1, one launch (start us, length us, event | category | flops | bytes accessed | tf_op | source)
XLA Modules:
  0.0 172.7 jit_solution(1768006277808666196)
XLA Ops:
  0.6 77.1 %gather_and_project.1 = (bf16[2,5376,512]{2,1,0:T(8,128)(2,1)}, bf16[5376,512]{1,0:T(8,128)(2,1)}, bf16[8,336,512]{2,1,0:T(8,128)(2,1)}, f32[512,1024]{1,0:T(8,1...) custom-call(bf16[512,5376]{1,0:T(8,128)(2,1)} %x_hbm.1, ...), custom_call_target="tpu_custom_call" | custom-call | tf_op jit(solution)/shard_map/gather_and_project/pallas_call | solution.py:557
  77.8 0.0 copy-start
  77.8 0.0 copy-start.2
  77.8 87.7 %attention_and_reductions.1 = (f32[2,336,512]{2,1,0:T(8,128)}, bf16[336,1024]{1,0:T(8,128)(2,1)}, f32[8,128]{1,0:T(8,128)}, f32[8,128]{1,0:T(8,128)}) custom-call(bf16[2,5376,512]{2,1,0:T(8,128)(2,1)} %get-tuple-element.21.w_hbm, bf16[5376,512]{1,0:T(8,128)(2,1)} %get-tuple-element.22.nt_hbm, bf16[8,336,512]{2,1,0:T(8,128)(2,1)} %get-tuple-element.23.nt_far_hbm, ...), custom_call_target="tpu_custom_call" | custom-call | tf_op jit(solution)/shard_map/attention_and_reductions/pallas_call | solution.py:327
  165.5 1.3 multiply_bitcast_fusion
  166.7 0.8 dynamic_slice.6
  167.5 0.0 copy-done
  167.5 0.0 copy-done.2
  167.5 0.0 copy-start.1
  167.5 2.6 %fusion.2 = bf16[672,512]{1,0:T(8,128)(2,1)} fusion(f32[2,336,512]{2,1,0:T(8,128)} %get-tuple-element.28, bf16[672,512]{1,0:T(8,128)(2,1)S(1)} %copy-done, f32[512]{0:T(512)S(1)} %get-tuple-element.35, f32[672]{0:T(1024)S(1)} %dynamic_slice.6, f32[512]{0:T(512)S(1)} %bitcast.25), kind=kLoop, calls=%fused_computation.3 | loop fusion | flops 2408448 | bytes 2759296 | tf_op jit(solution)/shard_map/convert_element_type | solution.py:628
  170.0 0.0 copy-start.3
  170.1 0.0 copy-done.1
  170.1 0.7 fusion.3
  170.8 0.8 slice.22
  171.6 0.0 copy-done.3
  171.6 0.6 dynamic_slice.7
  172.1 0.5 slice_bitcast_fusion.1
  (1 shorter events, 0.0 us)
Async XLA Ops:
  77.8 89.7 %copy-start = (bf16[672,512]{1,0:T(8,128)(2,1)S(1)}, bf16[672,512]{1,0:T(8,128)(2,1)}, u32[]{:S(2)}) copy-start(bf16[672,512]{1,0:T(8,128)(2,1)} %get-tuple-element.27.x_mine_hbm) | copy-start | bytes 2064388
  77.8 89.7 %copy-start.2 = (f32[1,512]{1,0:T(1,128)S(1)}, f32[1,512]{1,0:T(1,128)}, u32[]{:S(2)}) copy-start(f32[1,512]{1,0:T(1,128)} %get-tuple-element.20.inv) | copy-start | bytes 6148
  167.5 2.6 %copy-start.1 = (bf16[336,1024]{1,0:T(8,128)(2,1)S(1)}, bf16[336,1024]{1,0:T(8,128)(2,1)}, u32[]{:S(2)}) copy-start(bf16[336,1024]{1,0:T(8,128)(2,1)} %get-tuple-element.30) | copy-start | bytes 2064388
  170.0 1.5 copy-start.3
